TPU v7x, 256 devices: a whole 4x4x8 slice. The times are simulated.
256 devices in a mesh: grp: 8 (over x, core), tile: 32 (over z, y).
Axes of the slice: x: 4, y: 4, z: 8, core: 2. Of those that a mesh axis runs over, the one named last changes fastest.
Arguments:
- features: bfloat16 [65536, 1024], P(('grp', 'tile'))
- projection: bfloat16 [1024, 768], replicated, may hold values from -0.1875 to 0.1875
- pooled_grad: bfloat16 [96, 768, 768], P('grp', 'tile'), may hold values from -96 to 96
- slide_counts: int32 [96], P('grp'), may hold values from 321 to 2176, as said below
- slide_offsets: int32 [96], P('grp'), may hold values from 0 to 7808, as said below
Outputs:
- feature_grad: bfloat16 [65536, 1024], P(('grp', 'tile'))
- projection_grad: float32 [1024, 768], replicated
Inputs may be any that keep to these rules, and one draw needn't show every extreme that they name: Within each group the slides lie end to end from row 0 and fill all 8192 rows in order; each slide spans a multiple of 128 rows, at least 384, and the last slide of each group exactly 384; slide_offsets gives each slide's first row within its group. A slide's first slide_counts rows are tiles, the rest of its span, fewer than 64 rows, is padding; a largest slide of each group, never the last, has no padding.
All inputs are finite; a program needn't handle non-finite values.
Results may differ from a plain program's by a relative error of at most 0.011.
Values may be sent and summed in bfloat16 or wider, within the bound.
No kernel may reach another device: no remote copies, remote signals or barrier semaphores. Data moves between devices by JAX's collectives and lax.ppermute only.
A program may use at most 256 MiB of HBM per device.

v0:
```python
import jax
import jax.numpy as jnp
from jax import lax
from jax.sharding import PartitionSpec as P

BLOCK = 128


def entering(value, axis, join, neutral):
    count = lax.axis_size(axis)
    place = lax.axis_index(axis)
    ahead = count - 1 - place
    gathered = jax.tree.map(
        lambda a, kind: lax.all_gather(a.astype(kind), axis),
        value,
        (jnp.bfloat16, jnp.bfloat16, jnp.bfloat16),
    )
    state = jax.tree.map(lambda a, e: jnp.zeros_like(a) + jnp.asarray(e, a.dtype), value, neutral)

    def entering_one(lap, state):
        source = count - 1 - lap
        return join(
            state,
            jax.tree.map(
                lambda a, own: lax.dynamic_index_in_dim(a, source, 0, False).astype(own.dtype),
                gathered,
                value,
            ),
        )

    return lax.fori_loop(0, ahead, entering_one, state)


def prefix(value, axis, join, neutral):
    place = lax.axis_index(axis)
    gathered = jax.tree.map(
        lambda a, kind: lax.all_gather(a.astype(kind), axis),
        value,
        jax.tree.map(lambda a: jnp.bfloat16 if a.dtype == jnp.float32 else a.dtype, value),
    )
    state = jax.tree.map(lambda a, e: jnp.zeros_like(a) + jnp.asarray(e, a.dtype), value, neutral)

    def prefix_one(lap, state):
        return join(
            state,
            jax.tree.map(
                lambda a, own: lax.dynamic_index_in_dim(a, lap, 0, False).astype(own.dtype),
                gathered,
                value,
            ),
        )

    return lax.fori_loop(0, place, prefix_one, state)


def pool_backward(sq_sum, row_sum, count, grads):
    mean_vec = row_sum / count
    covar = sq_sum / count - mean_vec[:, None] * mean_vec[None, :]
    norm_value = jnp.sqrt(jnp.sum(covar * covar) + 1e-06)
    scaled = covar / norm_value
    scaled_b = scaled.astype(jnp.bfloat16)
    first_iter = 1.5 * scaled - 0.5 * jnp.dot(
        scaled_b, scaled_b, preferred_element_type=jnp.float32
    )
    first_b = first_iter.astype(jnp.bfloat16)
    second_iter = 1.5 * first_iter - 0.5 * jnp.dot(
        scaled_b, first_b, preferred_element_type=jnp.float32
    )
    second_b = second_iter.astype(jnp.bfloat16)
    grad_top = jnp.sqrt(norm_value) * grads.astype(jnp.float32)
    grad_top_b = grad_top.astype(jnp.bfloat16)
    right_term = jnp.dot(grad_top_b, second_b.T, preferred_element_type=jnp.float32)
    grad_second = -0.5 * jnp.dot(first_b.T, grad_top_b, preferred_element_type=jnp.float32)
    grad_second_b = grad_second.astype(jnp.bfloat16)
    grad_first = (
        1.5 * grad_top
        - 0.5 * right_term
        + 1.5 * grad_second
        - 0.5 * jnp.dot(scaled_b.T, grad_second_b, preferred_element_type=jnp.float32)
    )
    grad_first_b = grad_first.astype(jnp.bfloat16)
    grad_scaled = (
        -0.5 * jnp.dot(grad_second_b, first_b.T, preferred_element_type=jnp.float32)
        + 1.5 * grad_first
    )
    grad_scaled = grad_scaled - 0.5 * (
        jnp.dot(grad_first_b, scaled_b.T, preferred_element_type=jnp.float32)
        + jnp.dot(scaled_b.T, grad_first_b, preferred_element_type=jnp.float32)
    )
    grad_norm = (
        1.5 * jnp.sum(grad_top * first_iter)
        - 0.5 * jnp.sum(right_term * first_b.astype(jnp.float32))
    ) / (2.0 * norm_value)
    grad_norm = grad_norm - jnp.sum(grad_scaled * scaled) / norm_value
    grad_covar = (grad_scaled + grad_norm * covar) / norm_value
    sym_grad = (grad_covar + grad_covar.T) / count
    mean_grad = -jnp.dot(sym_grad, mean_vec, precision=lax.Precision.HIGHEST)
    return (sym_grad.astype(jnp.bfloat16), mean_grad)


def pack_sym(full):
    half = full.shape[0] // 2
    upper = full[:half, :half]
    cross = full[half:, :half]
    lower = full[half:, half:]
    row_ids = jnp.arange(half, dtype=jnp.int32)[:, None]
    col_ids = jnp.arange(half, dtype=jnp.int32)[None, :]
    folded = jnp.where(row_ids >= col_ids, upper, lower.T)
    return jnp.concatenate([cross, folded, jnp.diagonal(lower)[None, :]], axis=0)


def unpack_sym(packed):
    half = packed.shape[1]
    cross = packed[:half]
    folded = packed[half : 2 * half]
    lower_diag = packed[2 * half]
    row_ids = jnp.arange(half, dtype=jnp.int32)[:, None]
    col_ids = jnp.arange(half, dtype=jnp.int32)[None, :]
    upper = jnp.where(row_ids >= col_ids, folded, folded.T)
    lower = jnp.where(
        row_ids > col_ids, folded.T, jnp.where(row_ids < col_ids, folded, lower_diag[None, :])
    )
    top = jnp.concatenate([upper, cross.T], axis=1)
    bottom = jnp.concatenate([cross, lower], axis=1)
    return jnp.concatenate([top, bottom], axis=0)


def add_chain(earlier, later):
    return (
        later[0] + later[2] * earlier[0],
        later[1] + later[2] * earlier[1],
        earlier[2] * later[2],
    )


def keep_nearest(earlier, later):
    passing = later[2] > 0.5
    return (
        jnp.where(passing, earlier[0], later[0]),
        jnp.where(passing, earlier[1], later[1]),
        earlier[2] * later[2],
    )


def shards(features, projection, pooled_grad, slide_counts, slide_offsets):
    tile_count = lax.axis_size("tile")
    rows = features.shape[0]
    width = projection.shape[1]
    block_count = rows // BLOCK
    slide_total = slide_offsets.shape[0]
    group_rows = rows * tile_count
    first_row = lax.axis_index("tile") * rows
    slide_ends = jnp.concatenate([slide_offsets[1:], jnp.full((1,), group_rows, jnp.int32)])

    def slide_of(places):
        return jnp.sum((slide_offsets[None, :] <= places[:, None]).astype(jnp.int32), axis=1) - 1

    positions = first_row + jnp.arange(rows, dtype=jnp.int32)
    row_slide = slide_of(positions)
    one_hot = (row_slide[:, None] == jnp.arange(slide_total, dtype=jnp.int32)[None, :]).astype(
        jnp.int32
    )
    row_start = jnp.sum(one_hot * slide_offsets[None, :], axis=1)
    row_limit = jnp.sum(one_hot * slide_counts[None, :], axis=1)
    valid = positions - row_start < row_limit
    edge_slides = slide_of(jnp.stack([first_row, first_row + rows - 1]))
    slot_first = edge_slides[0]
    slot_last = edge_slides[1]
    same_slide = slot_first == slot_last
    from_left = slide_offsets[slot_first] < first_row
    to_right = slide_ends[slot_last] > first_row + rows
    owns = slide_offsets[slot_last] >= first_row
    passing = (same_slide & from_left & to_right).astype(jnp.float32)
    count_real = slide_counts.astype(jnp.float32)
    mixed = jnp.dot(features, projection, preferred_element_type=jnp.float32).astype(jnp.bfloat16)
    masked = jnp.where(valid[:, None], mixed, jnp.zeros((), jnp.bfloat16))
    blocks = masked.reshape(block_count, BLOCK, width)
    block_second = row_slide.reshape(block_count, BLOCK)[:, 0] != slot_first
    second_weight = block_second.astype(jnp.float32)
    first_weight = 1.0 - second_weight
    block_sum = jnp.sum(blocks, axis=1, dtype=jnp.float32)
    first_blocks = jnp.where(
        block_second[:, None, None], jnp.zeros((), jnp.bfloat16), blocks
    ).reshape(rows, width)
    last_blocks = jnp.where(
        block_second[:, None, None], blocks, jnp.zeros((), jnp.bfloat16)
    ).reshape(rows, width)
    part_sq_first = pack_sym(
        jnp.einsum("rd,re->de", first_blocks, first_blocks, preferred_element_type=jnp.float32)
    )
    part_sq_last = pack_sym(
        jnp.einsum("rd,re->de", last_blocks, last_blocks, preferred_element_type=jnp.float32)
    )
    part_sum_first = jnp.sum(first_weight[:, None] * block_sum, axis=0)
    part_sum_last = jnp.sum(second_weight[:, None] * block_sum, axis=0)
    right_sq = jnp.where(same_slide, part_sq_first, part_sq_last)
    right_sum = jnp.where(same_slide, part_sum_first, part_sum_last)
    zero_sq = jnp.zeros(part_sq_first.shape, jnp.float32)
    zero_sum = jnp.zeros((width,), jnp.float32)
    tail_sq, tail_sum, tail_flag = entering(
        (
            jnp.where(from_left, part_sq_first, 0.0),
            jnp.where(from_left, part_sum_first, 0.0),
            passing,
        ),
        "tile",
        add_chain,
        (zero_sq, zero_sum, jnp.float32(1.0)),
    )
    zero_q = jnp.zeros((width, width), jnp.bfloat16)
    zero_packed = jnp.zeros(part_sq_first.shape, jnp.bfloat16)
    owner_device = slide_offsets // rows
    owner_match = (
        owner_device[None, :] == jnp.arange(tile_count, dtype=jnp.int32)[:, None]
    ).astype(jnp.int32)
    owned_index = jnp.sum(owner_match * jnp.arange(slide_total, dtype=jnp.int32)[None, :], axis=1)
    outgoing = jnp.take(pooled_grad, owned_index, axis=0).reshape(width, width)
    grad_owned = lax.all_to_all(outgoing, "tile", split_axis=0, concat_axis=0, tiled=True)
    total_sq = unpack_sym(right_sq + tail_sq)
    total_sum = right_sum + tail_sum
    owned_q, owned_mean = lax.cond(
        owns,
        lambda: pool_backward(total_sq, total_sum, count_real[slot_last], grad_owned),
        lambda: (zero_q, zero_sum),
    )
    owned_packed = pack_sym(owned_q)
    given_packed, given_mean, given_flag = prefix(
        (owned_packed, owned_mean, passing),
        "tile",
        keep_nearest,
        (zero_packed, zero_sum, jnp.float32(1.0)),
    )
    given_q = unpack_sym(given_packed)
    q_first = jnp.where(from_left, given_q, owned_q)
    mean_first = jnp.where(from_left, given_mean, owned_mean)
    q_last = jnp.where(owns, owned_q, given_q)
    mean_last = jnp.where(owns, owned_mean, given_mean)
    first_grad = jnp.dot(first_blocks, q_first, preferred_element_type=jnp.float32)
    last_grad = jnp.dot(last_blocks, q_last, preferred_element_type=jnp.float32)
    row_second = jnp.repeat(second_weight, BLOCK)[:, None]
    row_mean = (1.0 - row_second) * mean_first[None, :] + row_second * mean_last[None, :]
    row_grad = jnp.where(valid[:, None], first_grad + last_grad + row_mean, 0.0).astype(
        jnp.bfloat16
    )
    feature_grad = jnp.einsum(
        "rd,kd->rk", row_grad, projection, preferred_element_type=jnp.float32
    ).astype(jnp.bfloat16)
    local_term = jnp.einsum("rk,rd->kd", features, row_grad, preferred_element_type=jnp.float32)
    projection_grad = lax.psum(local_term, ("grp", "tile"))
    return (feature_grad, projection_grad)


def solution(mesh):
    placed = (P(("grp", "tile"), None), P(), P("grp", "tile", None), P("grp"), P("grp"))
    return jax.shard_map(
        shards,
        mesh=mesh,
        in_specs=placed,
        out_specs=(P(("grp", "tile"), None), P()),
        check_vma=False,
    )
```

profile of v0, /device:TPU:1, one launch (start us, length us, event | category | flops | bytes accessed | tf_op | source)
XLA Modules:
  0.0 867.5 jit_solution(8792908519203807564)
XLA Ops:
  21.8 3.5 gather_fusion
  29.7 1.6 gather_fusion.2
  33.3 12.3 %all-to-all-start = ((bf16[32,24,768]{2,1,0:T(8,128)(2,1)}), bf16[32,24,768]{2,1,0:T(8,128)(2,1)}, u32[]{:S(2)}, u32[]{:S(2)}) async-start(bf16[32,24,768]{2,1,0:T(8,128)(2,1)} %broadcast_select_fusion.1), calls=%async_computation | async-start | bytes 2359296 | tf_op jit(solution)/shard_map/all_to_all | solution.py:218
  45.7 88.4 %all-reduce = bf16[32]{0:T(256)(128)(2,1)S(1)} all-reduce(bf16[32]{0:T(256)(128)(2,1)S(1)} %dynamic-update-slice), channel_id=1, replica_groups=mesh['grp'=8,'tile'=32] {'tile'}, use_global_device_ids=true, to_apply=%add | all-reduce | flops 32 | bytes 128
  134.3 37.1 %all-gather.3 = bf16[32,1,768]{2,1,0:T(2,128)(2,1)S(1)} all-gather(bf16[1,1,768]{2,1,0:T(2,128)(2,1)S(1)} %reshape.201), channel_id=2, replica_groups=mesh['grp'=8,'tile'=32] {'tile'}, dimensions={0}, use_global_device_ids=true | all-gather | bytes 50688 | tf_op jit(solution)/shard_map/all_gather | solution.py:14
  173.9 3.5 gather_fusion.1
  178.1 2.0 slice_select_fusion
  180.0 26.0 %all-gather.9.cloned.1.call-done = bf16[32,769,384]{2,1,0:T(8,128)(2,1)} async-done(((bf16[1,769,384]{2,1,0:T(8,128)(2,1)}), bf16[32,769,384]{2,1,0:T(8,128)(2,1)}) %all-gather.9.cloned.1.call-update) | async-done | bytes 18898960 | tf_op jit(solution)/shard_map/all_gather | solution.py:14
  206.2 88.0 %while.30 = (s32[]{:T(128)}, f32[769,384]{1,0:T(8,128)S(1)}, f32[768]{0:T(1024)S(1)}, s32[]{:T(128)}, bf16[32,769,384]{2,1,0:T(8,128)(2,1)}, /*index=5*/bf16[32]...) while((s32[]{:T(128)}, f32[769,384]{1,0:T(8,128)S(1)}, ...), condition=%wide.region_7.8_spmd, body=%wide.region_6.7_spmd.sunk | while | flops 888199 | bytes 2966969 | solution.py:31
  294.1 1.7 fusion.27
  297.9 2.2 bitcast_select_fusion.2
  300.3 2.6 maximum_maximum_fusion
  303.0 58.4 %conditional.1 = (bf16[768,768]{1,0:T(8,128)(2,1)}, f32[768]{0:T(1024)S(1)}, bf16[384,384]{1,0:T(8,128)(2,1)S(1)}, bf16[384,384]{1,0:T(8,128)(2,1)S(1)}, bf16[384,384]{1,0:T(8,128)(2,1)S(1)}) conditional(s32[]{:T(128)} %convert_element_type.144, () %tuple.40, (s32[]{:T(128)}, f32[12]{0:T(128)S(1)}, f32[768,768]{1,0:T(8,128)}, pred[]{:T(512)}, ...), branch_computations={%region_9.10_spmd, %region_10.16_spmd} | conditional | flops 7305565184 | bytes 163443232 | solution.py:221
  306.2 3.8 multiply_reduce_fusion.2
  312.8 4.5 fusion.4
  318.5 2.5 fusion.5
  321.1 7.9 multiply_reduce_fusion.1
  329.0 6.6 fusion.3
  335.7 2.0 fusion.8
  337.7 4.5 multiply_reduce_fusion
  344.1 4.9 add_divide_fusion
  349.0 3.1 copy.161
  352.1 4.9 fusion.15
  358.2 2.8 convolution_reduce_fusion
  361.6 3.7 gather_fusion.3
  367.6 33.1 %all-gather.5 = bf16[32,1,768]{2,1,0:T(2,128)(2,1)S(1)} all-gather(bf16[1,1,768]{2,1,0:T(2,128)(2,1)S(1)} %reshape.205), channel_id=4, replica_groups=mesh['grp'=8,'tile'=32] {'tile'}, dimensions={0}, use_global_device_ids=true | all-gather | bytes 50688 | tf_op jit(solution)/shard_map/all_gather | solution.py:37
  400.8 111.4 %all-gather.11.cloned.1.call-done = bf16[32,769,384]{2,1,0:T(8,128)(2,1)} async-done(((bf16[1,769,384]{2,1,0:T(8,128)(2,1)}), bf16[32,769,384]{2,1,0:T(8,128)(2,1)}) %all-gather.11.cloned.1.call-update) | async-done | bytes 18898960 | tf_op jit(solution)/shard_map/all_gather | solution.py:37
  514.7 1.9 fusion.30
  516.6 2.0 fusion.25
  518.6 2.3 convolution_bitcast_fusion
  522.3 335.1 %all-reduce.3.cloned.1.call-done = f32[1024,768]{0,1:T(8,128)} async-done(((f32[1024,768]{0,1:T(8,128)}), f32[1024,768]{0,1:T(8,128)}) %all-reduce.3.cloned.1.call-update) | async-done | bytes 3145744 | tf_op jit(solution)/shard_map/psum | solution.py:249
  857.5 3.5 copy.173
  (269 shorter events, 98.3 us)
Async XLA Ops:
  7.2 6.6 copy-start
  7.2 198.9 %all-gather.9.cloned.1.call-start = ((), (), s32[]{:S(2)}) async-start(), calls=%async_computation.1 | async-start | bytes 19666944 | tf_op jit(solution)/shard_map/all_gather | solution.py:14
  13.0 158.5 %copy-start.20 = (pred[256]{0:T(512)(128)(4,1)}, pred[256]{0:T(512)(128)(4,1)S(1)}, u32[]{:S(2)}) copy-start(pred[256]{0:T(512)(128)(4,1)S(1)} %broadcast_bitcast_fusion) | copy-start | bytes 772
  13.8 2.3 copy-start.22
  15.4 1.7 copy-start.11
  16.0 1.8 copy-start.6
  17.1 3.4 copy-start.18
  18.1 7.3 copy-start.14
  19.2 9.7 %copy-start.25 = (u32[256]{0:T(256)S(1)}, u32[256]{0:T(256)}, u32[]{:S(2)}) copy-start(u32[256]{0:T(256)} %constant.202) | copy-start | bytes 3076
  32.1 101.9 %copy-start.24 = (s32[12]{0:T(128)S(1)}, s32[12]{0:T(128)}, u32[]{:S(2)}) copy-start(s32[12]{0:T(128)} %param.14) | copy-start | bytes 148
  33.3 138.1 %copy-start.12 = (bf16[256,768]{1,0:T(8,128)(2,1)S(1)}, bf16[256,768]{1,0:T(8,128)(2,1)}, u32[]{:S(2)}) copy-start(bf16[256,768]{1,0:T(8,128)(2,1)} %copy-done.11) | copy-start | bytes 1179652
  33.3 269.7 %all-to-all-start = ((bf16[32,24,768]{2,1,0:T(8,128)(2,1)}), bf16[32,24,768]{2,1,0:T(8,128)(2,1)}, u32[]{:S(2)}, u32[]{:S(2)}) async-start(bf16[32,24,768]{2,1,0:T(8,128)(2,1)} %broadcast_select_fusion.1), calls=%async_computation | async-start | bytes 2359296 | tf_op jit(solution)/shard_map/all_to_all | solution.py:218
  45.6 466.6 %all-gather.11.cloned.1.call-start = ((), (), s32[]{:S(2)}) async-start(), calls=%async_computation.3 | async-start | bytes 19666944 | tf_op jit(solution)/shard_map/all_gather | solution.py:37
  172.1 1.6 copy-start.8
  295.8 1.0 copy-start.7
  310.8 2.0 copy-start.2
  312.8 4.5 copy-start.5
  317.3 1.2 copy-start.15
  318.5 2.5 copy-start.10
  329.0 6.6 copy-start.3
  335.7 2.0 copy-start.9
  352.1 6.1 copy-start.1
  352.1 6.1 copy-start.4
  366.2 491.3 %all-reduce.3.cloned.1.call-start = ((), (), s32[]{:S(2)}) async-start(), calls=%async_computation.2 | async-start | bytes 6291456 | tf_op jit(solution)/shard_map/psum | solution.py:249
  512.3 2.3 copy-start.13
  513.2 1.2 copy-start.19
  514.6 2.0 copy-start.17
  514.6 2.0 copy-start.21
  514.6 2.0 copy-start.23
  514.6 2.0 copy-start.26
  514.6 2.0 copy-start.27
  516.6 2.0 copy-start.16
Sparse Core Ops, SparseCore 0:
  26.4 179.5 all-gather.8
  366.3 145.8 all-gather.10
  521.1 336.3 all-reduce.2
where the time goes:
time: 871 us; the launch traced here: 868 us
  waiting for transfers between devices  473 us (54%)
  blocking collectives  159 us (18%)
  other arithmetic  81.4 us (9%)
  local copies, waits for them, and re-layouts  52.3 us (6%)
  matrix products  42.5 us (5%)
  loops' own time  26.5 us (3%)
  between operations  21.2 us (2%)
  starting transfers between devices  12.4 us (1%)
    psum x1, waiting for transfers between devices, shards(): projection_grad = lax.psum(local_term, ('grp', 'tile'))  335 us
    all_gather x1, waiting for transfers between devices, prefix(): lax.all_gather(a.astype(kind), axis)  111 us
    unnamed x1, blocking collectives  88.4 us
    add x31, other arithmetic, add_chain(): later[0] + later[2] * earlier[0]  47.3 us
    all_gather x1, blocking collectives, entering(): lax.all_gather(a.astype(kind), axis)  37.1 us
    all_gather x1, blocking collectives, prefix(): lax.all_gather(a.astype(kind), axis)  33.1 us
    all_gather x1, waiting for transfers between devices, entering(): lax.all_gather(a.astype(kind), axis)  26 us
    another operation x1, loops' own time, entering(): return lax.fori_loop(0, ahead, entering_one, state)  21.6 us
  transfers between devices with their start and end apart: 4, of which 3 were waited for; matrix products, arithmetic and copies ran while one was open for 10% of the time, Pallas kernels for 0%

commit v1 on v0

--- a/solution.py
+++ b/solution.py
@@ -140,6 +140,64 @@
         jnp.where(passing, earlier[1], later[1]),
         earlier[2] * later[2],
     )
+
+CORE_PAIRS = [(i, i ^ 1) for i in range(8)]
+
+
+def x_shift(step):
+    return [(x * 2 + c, (x + step) % 4 * 2 + c) for x in range(4) for c in range(2)]
+
+
+def y_shift(step):
+    return [(z * 4 + y, z * 4 + (y + step) % 4) for z in range(8) for y in range(4)]
+
+
+Z_GROUPS = [[z * 4 + y for z in range(8)] for y in range(4)]
+
+
+def scatter_four(value, axis, shift, place):
+    rows = value.shape[0] // 4
+    parts = value.reshape(4, rows, value.shape[1])
+    sent = parts.astype(jnp.bfloat16)
+    got = [
+        lax.ppermute(lax.dynamic_index_in_dim(sent, (place + step) % 4, 0, False), axis, shift(step))
+        for step in (1, 3, 2)
+    ]
+    total = lax.dynamic_index_in_dim(parts, place, 0, False)
+    for one in got:
+        total = total + one.astype(jnp.float32)
+    return total
+
+
+def gather_four(value, axis, shift, place):
+    out = jnp.zeros((4,) + value.shape, value.dtype)
+    got = [(step, lax.ppermute(value, axis, shift(step))) for step in (1, 3, 2)]
+    out = lax.dynamic_update_index_in_dim(out, value, place, 0)
+    for step, one in got:
+        out = lax.dynamic_update_index_in_dim(out, one, (place - step) % 4, 0)
+    return out.reshape(4 * value.shape[0], value.shape[1])
+
+
+def reduce_everywhere(term):
+    group = lax.axis_index("grp")
+    core = group % 2
+    x_place = group // 2
+    y_place = lax.axis_index("tile") % 4
+    halves = term.reshape(2, term.shape[0] // 2, term.shape[1])
+    other = lax.dynamic_index_in_dim(halves, 1 - core, 0, False).astype(jnp.bfloat16)
+    mine = lax.dynamic_index_in_dim(halves, core, 0, False)
+    total = mine + lax.ppermute(other, "grp", CORE_PAIRS).astype(jnp.float32)
+    total = scatter_four(total, "grp", x_shift, x_place)
+    total = scatter_four(total, "tile", y_shift, y_place)
+    sent = jnp.broadcast_to(total.astype(jnp.bfloat16)[None], (8,) + total.shape)
+    got = lax.all_to_all(sent, "tile", 0, 0, axis_index_groups=Z_GROUPS, tiled=True)
+    value = jnp.sum(got.astype(jnp.float32), axis=0).astype(jnp.bfloat16)
+    value = gather_four(value, "tile", y_shift, y_place)
+    value = gather_four(value, "grp", x_shift, x_place)
+    theirs = lax.ppermute(value, "grp", CORE_PAIRS)
+    low = jnp.where(core == 0, value, theirs)
+    high = jnp.where(core == 0, theirs, value)
+    return jnp.concatenate([low, high], axis=0).astype(jnp.float32)
 
 
 def shards(features, projection, pooled_grad, slide_counts, slide_offsets):
@@ -246,7 +304,7 @@
         "rd,kd->rk", row_grad, projection, preferred_element_type=jnp.float32
     ).astype(jnp.bfloat16)
     local_term = jnp.einsum("rk,rd->kd", features, row_grad, preferred_element_type=jnp.float32)
-    projection_grad = lax.psum(local_term, ("grp", "tile"))
+    projection_grad = reduce_everywhere(local_term)
     return (feature_grad, projection_grad)
 
 

time: 871 us -> 698 us (0.80)
  waiting for transfers between devices: 473 us -> 172 us
  starting transfers between devices: 12.4 us -> 112 us
  local copies, waits for them, and re-layouts: 52.3 us -> 69.3 us
    psum x1 -> x0, waiting for transfers between devices: 335 us -> none  [shards(): projection_grad = lax.psum(local_term, ('grp', 'tile'))]
    all_to_all x0 -> x1, starting transfers between devices: none -> 72.2 us  [reduce_everywhere(): lax.all_to_all(sent, 'tile', 0, 0, axis_index_groups=Z_GROUPS, tiled=True)]
    ppermute x0 -> x14, starting transfers between devices: none -> 27.3 us  [the longest x6 13.5 us: scatter_four(): lax.ppermute(lax.dynamic_index_in_dim(sent, (place + step) % 4, 0, False)...]
    ppermute x0 -> x14, waiting for transfers between devices: none -> 22.4 us  [the longest x6 11.7 us: scatter_four(): lax.ppermute(lax.dynamic_index_in_dim(sent, (place + step) % 4, 0, False)...]
    all_to_all x0 -> x1, waiting for transfers between devices: none -> 11.9 us  [reduce_everywhere(): lax.all_to_all(sent, 'tile', 0, 0, axis_index_groups=Z_GROUPS, tiled=True)]
    dynamic_slice x0 -> x3, local copies, waits for them, and re-layouts: none -> 9.58 us  [the longest x2 6.28 us: reduce_everywhere(): mine = lax.dynamic_index_in_dim(halves, core, 0, False)]
  transfers between devices with their start and end apart: 4 -> 18, of which waited for: 3 -> 13; matrix products, arithmetic and copies ran while one was open for 10% -> 14% of each run, Pallas kernels for 0% -> 0%
where the time goes in v1:
time: 698 us; the launch traced here: 689 us
  waiting for transfers between devices  172 us (25%)
  blocking collectives  159 us (23%)
  starting transfers between devices  112 us (16%)
  other arithmetic  86.4 us (12%)
  local copies, waits for them, and re-layouts  69.3 us (10%)
  matrix products  42.8 us (6%)
  loops' own time  26.5 us (4%)
  between operations  22 us (3%)
    all_gather x1, waiting for transfers between devices, prefix(): lax.all_gather(a.astype(kind), axis)  111 us
    unnamed x1, blocking collectives  88.4 us
    all_to_all x1, starting transfers between devices, reduce_everywhere(): lax.all_to_all(sent, 'tile', 0, 0, axis_index_groups=Z_GROUPS, tiled=True)  72.2 us
    add x31, other arithmetic, add_chain(): later[0] + later[2] * earlier[0]  47.3 us
    all_gather x1, blocking collectives, entering(): lax.all_gather(a.astype(kind), axis)  37.1 us
    all_gather x1, blocking collectives, prefix(): lax.all_gather(a.astype(kind), axis)  33.4 us
    all_gather x1, waiting for transfers between devices, entering(): lax.all_gather(a.astype(kind), axis)  26.2 us
    another operation x1, loops' own time, entering(): return lax.fori_loop(0, ahead, entering_one, state)  21.6 us
  transfers between devices with their start and end apart: 18, of which 13 were waited for; matrix products, arithmetic and copies ran while one was open for 14% of the time, Pallas kernels for 0%

profile of v1, /device:TPU:1, one launch (start us, length us, event | category | flops | bytes accessed | tf_op | source)
XLA Modules:
  0.0 689.5 jit_solution(16893013669587788169)
XLA Ops:
  21.8 3.5 gather_fusion
  33.2 12.3 %all-to-all-start = ((bf16[32,24,768]{2,1,0:T(8,128)(2,1)}), bf16[32,24,768]{2,1,0:T(8,128)(2,1)}, u32[]{:S(2)}, u32[]{:S(2)}) async-start(bf16[32,24,768]{2,1,0:T(8,128)(2,1)} %broadcast_select_fusion.1), calls=%async_computation | async-start | bytes 2359296 | tf_op jit(solution)/shard_map/all_to_all | solution.py:276
  45.5 88.4 %all-reduce = bf16[32]{0:T(256)(128)(2,1)S(1)} all-reduce(bf16[32]{0:T(256)(128)(2,1)S(1)} %dynamic-update-slice), channel_id=1, replica_groups=mesh['grp'=8,'tile'=32] {'tile'}, use_global_device_ids=true, to_apply=%add | all-reduce | flops 32 | bytes 128
  134.2 37.1 %all-gather.3 = bf16[32,1,768]{2,1,0:T(2,128)(2,1)S(1)} all-gather(bf16[1,1,768]{2,1,0:T(2,128)(2,1)S(1)} %reshape.224), channel_id=2, replica_groups=mesh['grp'=8,'tile'=32] {'tile'}, dimensions={0}, use_global_device_ids=true | all-gather | bytes 50688 | tf_op jit(solution)/shard_map/all_gather | solution.py:14
  173.8 3.5 gather_fusion.1
  179.8 26.2 %all-gather.9.cloned.1.call-done = bf16[32,769,384]{2,1,0:T(8,128)(2,1)} async-done(((bf16[1,769,384]{2,1,0:T(8,128)(2,1)}), bf16[32,769,384]{2,1,0:T(8,128)(2,1)}) %all-gather.9.cloned.1.call-update) | async-done | bytes 18898960 | tf_op jit(solution)/shard_map/all_gather | solution.py:14
  206.1 87.9 %while.30 = (s32[]{:T(128)}, f32[769,384]{1,0:T(8,128)S(1)}, f32[768]{0:T(1024)S(1)}, s32[]{:T(128)}, bf16[32,769,384]{2,1,0:T(8,128)(2,1)}, /*index=5*/bf16[32]...) while((s32[]{:T(128)}, f32[769,384]{1,0:T(8,128)S(1)}, ...), condition=%wide.region_7.8_spmd, body=%wide.region_6.7_spmd.sunk | while | flops 888199 | bytes 2966969 | solution.py:31
  302.7 58.7 %conditional.1 = (bf16[768,768]{1,0:T(8,128)(2,1)}, f32[768]{0:T(1024)S(1)}, bf16[384,384]{1,0:T(8,128)(2,1)S(1)}, bf16[384,384]{1,0:T(8,128)(2,1)S(1)}, bf16[384,384]{1,0:T(8,128)(2,1)S(1)}) conditional(s32[]{:T(128)} %convert_element_type.185, () %tuple.40, (s32[]{:T(128)}, f32[12]{0:T(128)S(1)}, f32[768,768]{1,0:T(8,128)}, pred[]{:T(512)}, ...), branch_computations={%region_9.10_spmd, %region_10.16_spmd} | conditional | flops 7305565184 | bytes 163443232 | solution.py:279
  306.2 3.7 multiply_reduce_fusion.2
  312.6 4.3 fusion.4
  320.7 8.0 %multiply_reduce_fusion.1 = (f32[]{:T(128)}, f32[768,768]{1,0:T(8,128)}) fusion(bf16[768,768]{1,0:T(8,128)(2,1)} %copy-done.17, bf16[768,768]{1,0:T(8,128)(2,1)S(1)} %bitcast_convert_fusion, f32[768,768]{1,0:T(8,128)} %get-tuple-element.378, f32[]{:T(128)S(6)} %sqrt.4, f32[768]{0:T(1024)S(1)} %add_divide_fusion.1, f32[768,768]{1,0:T(8,128)} %get-tuple-element.189, ...), kind=kOutput, calls=%fused_computation.18 | convolution fusion | flops 1819017216 | bytes 9440268 | tf_op jit(solution)/shard_map/cond/branch_1_fun/dot_general | solution.py:72
  328.7 6.7 fusion.3
  337.5 4.7 multiply_reduce_fusion
  344.1 5.0 add_divide_fusion
  349.1 3.1 copy.167
  352.2 4.9 fusion.15
  361.6 3.7 gather_fusion.3
  367.6 33.4 %all-gather.5 = bf16[32,1,768]{2,1,0:T(2,128)(2,1)S(1)} all-gather(bf16[1,1,768]{2,1,0:T(2,128)(2,1)S(1)} %reshape.228), channel_id=4, replica_groups=mesh['grp'=8,'tile'=32] {'tile'}, dimensions={0}, use_global_device_ids=true | all-gather | bytes 50688 | tf_op jit(solution)/shard_map/all_gather | solution.py:37
  401.0 111.3 %all-gather.11.cloned.1.call-done = bf16[32,769,384]{2,1,0:T(8,128)(2,1)} async-done(((bf16[1,769,384]{2,1,0:T(8,128)(2,1)}), bf16[32,769,384]{2,1,0:T(8,128)(2,1)}) %all-gather.11.cloned.1.call-update) | async-done | bytes 18898960 | tf_op jit(solution)/shard_map/all_gather | solution.py:37
  521.2 5.6 reshape.182
  526.8 3.3 constant_dynamic-slice_fusion
  530.1 2.9 copy.185
  534.0 3.2 constant_dynamic-slice_fusion.1
  537.3 3.0 copy.179
  547.1 3.8 collective-permute-done.1
  551.6 4.6 collective-permute-done.3
  559.8 5.8 collective-permute-start.5
  567.0 3.1 collective-permute-done.6
  570.9 72.2 %all-to-all-start.1 = ((bf16[8,32,768]{2,1,0:T(8,128)(2,1)}), bf16[8,32,768]{2,1,0:T(8,128)(2,1)S(1)}, u32[]{:S(2)}, u32[]{:S(2)}) async-start(bf16[8,32,768]{2,1,0:T(8,128)(2,1)} %broadcast_in_dim.208), calls=%async_computation.1 | async-start | bytes 786432 | tf_op jit(solution)/shard_map/all_to_all | solution.py:193
  643.1 11.9 %all-to-all-done.1 = bf16[8,32,768]{2,1,0:T(8,128)(2,1)S(1)} async-done(((bf16[8,32,768]{2,1,0:T(8,128)(2,1)}), bf16[8,32,768]{2,1,0:T(8,128)(2,1)S(1)}, u32[]{:S(2)}, u32[]{:S(2)}) %all-to-all-start.1) | async-done | bytes 393248 | tf_op jit(solution)/shard_map/all_to_all | solution.py:193
  659.3 2.9 collective-permute-done.9
  671.0 7.3 %collective-permute-start.13 = (bf16[512,768]{1,0:T(8,128)(2,1)S(1)}, bf16[512,768]{1,0:T(8,128)(2,1)S(1)}, u32[]{:S(2)}, u32[]{:S(2)}) collective-permute-start(bf16[512,768]{1,0:T(8,128)(2,1)S(1)} %bitcast.159), channel_id=1, source_target_pairs={{0,32},{32,0},{64,96},{96,64},{128,160},{160,128},{192,224},{224,1... | collective-permute-start | bytes 2359304 | tf_op jit(solution)/shard_map/ppermute | solution.py:197
  (320 shorter events, 151.7 us)
Async XLA Ops:
  7.2 6.6 copy-start
  7.2 198.8 %all-gather.9.cloned.1.call-start = ((), (), s32[]{:S(2)}) async-start(), calls=%async_computation.2 | async-start | bytes 19666944 | tf_op jit(solution)/shard_map/all_gather | solution.py:14
  13.7 2.3 copy-start.22
  17.1 3.4 copy-start.21
  18.1 7.2 %copy-start.16 = (bf16[1,384,384]{2,1,0:T(8,128)(2,1)S(1)}, bf16[1,384,384]{2,1,0:T(8,128)(2,1)}, u32[]{:S(2)}) copy-start(bf16[1,384,384]{2,1,0:T(8,128)(2,1)} %slice_bitcast_fusion.1) | copy-start | bytes 884740
  19.2 9.6 %copy-start.25 = (u32[256]{0:T(256)S(1)}, u32[256]{0:T(256)}, u32[]{:S(2)}) copy-start(u32[256]{0:T(256)} %constant.349) | copy-start | bytes 3076
  32.0 102.0 %copy-start.24 = (s32[12]{0:T(128)S(1)}, s32[12]{0:T(128)}, u32[]{:S(2)}) copy-start(s32[12]{0:T(128)} %param.14) | copy-start | bytes 148
  33.2 138.2 %copy-start.14 = (bf16[256,768]{1,0:T(8,128)(2,1)S(1)}, bf16[256,768]{1,0:T(8,128)(2,1)}, u32[]{:S(2)}) copy-start(bf16[256,768]{1,0:T(8,128)(2,1)} %copy-done.13) | copy-start | bytes 1179652
  33.2 269.5 %all-to-all-start = ((bf16[32,24,768]{2,1,0:T(8,128)(2,1)}), bf16[32,24,768]{2,1,0:T(8,128)(2,1)}, u32[]{:S(2)}, u32[]{:S(2)}) async-start(bf16[32,24,768]{2,1,0:T(8,128)(2,1)} %broadcast_select_fusion.1), calls=%async_computation | async-start | bytes 2359296 | tf_op jit(solution)/shard_map/all_to_all | solution.py:276
  45.5 466.8 %all-gather.11.cloned.1.call-start = ((), (), s32[]{:S(2)}) async-start(), calls=%async_computation.3 | async-start | bytes 19666944 | tf_op jit(solution)/shard_map/all_gather | solution.py:37
  312.6 4.3 copy-start.5
  318.1 2.6 copy-start.10
  328.7 6.7 copy-start.3
  352.2 6.1 copy-start.1
  352.2 6.1 copy-start.4
  516.1 2.8 copy-start.18
  533.0 7.3 %collective-permute-start = (bf16[512,768]{1,0:T(8,128)(2,1)}, bf16[512,768]{1,0:T(8,128)(2,1)}, u32[]{:S(2)}, u32[]{:S(2)}) collective-permute-start(bf16[512,768]{1,0:T(8,128)(2,1)} %bitcast.167), channel_id=1, source_target_pairs={{0,32},{32,0},{64,96},{96,64},{128,160},{160,128},{192,224},{224,1... | collective-permute-start | bytes 2359304 | tf_op jit(solution)/shard_map/ppermute | solution.py:189
  542.9 8.0 %collective-permute-start.1 = (bf16[128,768]{1,0:T(8,128)(2,1)}, bf16[128,768]{1,0:T(8,128)(2,1)S(1)}, u32[]{:S(2)}, u32[]{:S(2)}) collective-permute-start(bf16[128,768]{1,0:T(8,128)(2,1)} %get-tuple-element.394), channel_id=1, source_target_pairs={{0,64},{32,96},{64,128},{96,160},{128,192},{160,224},{192,0},{224,... | collective-permute-start | bytes 589832 | tf_op jit(solution)/shard_map/ppermute | solution.py:163
  544.1 6.8 collective-permute-start.2
  545.6 10.5 %collective-permute-start.3 = (bf16[128,768]{1,0:T(8,128)(2,1)S(1)}, bf16[128,768]{1,0:T(8,128)(2,1)}, u32[]{:S(2)}, u32[]{:S(2)}) collective-permute-start(bf16[128,768]{1,0:T(8,128)(2,1)S(1)} %get-tuple-element.395), channel_id=1, source_target_pairs={{0,128},{32,160},{64,192},{96,224},{128,0},{160,32},{192,64},{224,... | collective-permute-start | bytes 589832 | tf_op jit(solution)/shard_map/ppermute | solution.py:163
  557.4 9.6 %collective-permute-start.4 = (bf16[32,768]{1,0:T(8,128)(2,1)S(1)}, bf16[32,768]{1,0:T(8,128)(2,1)S(1)}, u32[]{:S(2)}, u32[]{:S(2)}) collective-permute-start(bf16[32,768]{1,0:T(8,128)(2,1)S(1)} %get-tuple-element.400), channel_id=1, source_target_pairs={{0,1},{1,2},{2,3},{3,0},{4,5},{5,6},{6,7},{7,4},{8,9},{9,10},{10,1... | collective-permute-start | bytes 147464 | tf_op jit(solution)/shard_map/ppermute | solution.py:163
  559.8 7.2 %collective-permute-start.5 = (bf16[32,768]{1,0:T(8,128)(2,1)S(1)}, bf16[32,768]{1,0:T(8,128)(2,1)S(1)}, u32[]{:S(2)}, u32[]{:S(2)}) collective-permute-start(bf16[32,768]{1,0:T(8,128)(2,1)S(1)} %get-tuple-element.402), channel_id=1, source_target_pairs={{0,3},{1,0},{2,1},{3,2},{4,7},{5,4},{6,5},{7,6},{8,11},{9,8},{10,9... | collective-permute-start | bytes 147464 | tf_op jit(solution)/shard_map/ppermute | solution.py:163
  565.6 4.4 collective-permute-start.6
  570.1 108.1 %copy-start.12 = (bf16[256,768]{1,0:T(8,128)(2,1)S(1)}, bf16[256,768]{1,0:T(8,128)(2,1)}, u32[]{:S(2)}) copy-start(bf16[256,768]{1,0:T(8,128)(2,1)} %copy-done.11) | copy-start | bytes 1179652
  570.9 84.1 %all-to-all-start.1 = ((bf16[8,32,768]{2,1,0:T(8,128)(2,1)}), bf16[8,32,768]{2,1,0:T(8,128)(2,1)S(1)}, u32[]{:S(2)}, u32[]{:S(2)}) async-start(bf16[8,32,768]{2,1,0:T(8,128)(2,1)} %broadcast_in_dim.208), calls=%async_computation.1 | async-start | bytes 786432 | tf_op jit(solution)/shard_map/all_to_all | solution.py:193
  655.1 4.2 collective-permute-start.7
  655.1 4.1 collective-permute-start.8
  657.8 4.4 collective-permute-start.9
  662.3 5.7 collective-permute-start.10
  663.0 6.7 collective-permute-start.11
  664.9 6.0 collective-permute-start.12
  671.0 9.2 %collective-permute-start.13 = (bf16[512,768]{1,0:T(8,128)(2,1)S(1)}, bf16[512,768]{1,0:T(8,128)(2,1)S(1)}, u32[]{:S(2)}, u32[]{:S(2)}) collective-permute-start(bf16[512,768]{1,0:T(8,128)(2,1)S(1)} %bitcast.159), channel_id=1, source_target_pairs={{0,32},{32,0},{64,96},{96,64},{128,160},{160,128},{192,224},{224,1... | collective-permute-start | bytes 2359304 | tf_op jit(solution)/shard_map/ppermute | solution.py:197
  (14 other events, 22.5 us)
Sparse Core Ops, SparseCore 0:
  26.4 179.5 all-gather.8
  366.4 145.8 all-gather.10
